TPU v7x, 32 devices: a whole 2x2x4 slice. The times are simulated.
32 devices in a mesh: dp: 16 (over z, x, core), tensor: 2 (over y).
Axes of the slice: x: 2, y: 2, z: 4, core: 2. Of those that a mesh axis runs over, the one named last changes fastest.
Arguments:
- acts: bfloat16 [2048, 2048], P('dp', 'tensor'), may hold values from -54 to 54
- partner: bfloat16 [2048, 2048], P('dp', 'tensor'), may hold values from -54 to 54
- hidden: bfloat16 [14336, 2048], P('dp', 'tensor'), may hold values from -6 to 6
- down_weight: bfloat16 [14336, 2048], P('dp', 'tensor'), may hold values from -0.046875 to 0.046875
Outputs:
- grad_hidden: bfloat16 [14336, 2048], P('dp', 'tensor')
- grad_weight: float32 [14336, 2048], P('dp', 'tensor')
- cka: float32 [], replicated
All inputs are finite; a program needn't handle non-finite values.
Results may differ from a plain program's by a relative error of at most 0.0059.
Values may be sent and summed in bfloat16 or wider, within the bound.
A program may use at most 64 MiB of HBM per device.

v0:
```python
import jax
import jax.numpy as jnp
from jax import lax
from jax.sharding import PartitionSpec as P


def center_rows(values):
    floats = values.astype(jnp.float32)
    return (floats - jnp.mean(floats, axis=0, keepdims=True)).astype(jnp.bfloat16)


def token_gram(values):
    return lax.dot_general(
        values, values, (((1,), (1,)), ((), ())), preferred_element_type=jnp.float32
    )


def local(acts, partner, hidden, down_weight):
    rows = acts.shape[0]
    width = acts.shape[1] * lax.axis_size("tensor")
    total = rows * lax.axis_size("dp")
    scale = float(total * width)
    centered_x = center_rows(acts)
    centered_y = center_rows(partner)
    whole_x, whole_y = (
        lax.all_gather(centered_x, "tensor", axis=1, tiled=True),
        lax.all_gather(centered_y, "tensor", axis=1, tiled=True),
    )
    gram_x = token_gram(whole_x)
    gram_y = token_gram(whole_y)
    sxx, syy, sxy = lax.psum(
        (jnp.sum(gram_x * gram_x), jnp.sum(gram_y * gram_y), jnp.sum(gram_x * gram_y)), "dp"
    )
    root = jnp.sqrt(sxx * syy)
    cka = sxy / root
    ratio = sxy / sxx
    coef = -2.0 * scale / root
    mixed = gram_y - ratio * gram_x
    grad = (
        coef * jnp.dot(mixed, centered_x.astype(jnp.float32), precision=lax.Precision.HIGHEST)
    ).astype(jnp.bfloat16)
    columns = lax.all_gather(grad, "dp", axis=0, tiled=True)
    token_block = lax.all_to_all(columns, "tensor", split_axis=0, concat_axis=1, tiled=True)
    part_grad = token_block
    grad_hidden = lax.dot_general(
        lax.all_gather(down_weight, "tensor", axis=1, tiled=True),
        part_grad,
        (((1,), (1,)), ((), ())),
        preferred_element_type=jnp.float32,
    ).astype(jnp.bfloat16)
    part_grad = columns
    grad_weight = lax.dot_general(
        lax.all_gather(hidden, "tensor", axis=1, tiled=True),
        part_grad,
        (((1,), (0,)), ((), ())),
        preferred_element_type=jnp.float32,
    )
    return (grad_hidden, grad_weight, cka)


def solution(mesh):
    in_specs = (P("dp", "tensor"), P("dp", "tensor"), P("dp", "tensor"), P("dp", "tensor"))
    out_specs = (P("dp", "tensor"), P("dp", "tensor"), P())
    return jax.shard_map(local, mesh=mesh, in_specs=in_specs, out_specs=out_specs, check_vma=False)
```

profile of v0, /device:TPU:0, one launch (start us, length us, event | category | flops | bytes accessed | tf_op | source)
XLA Modules:
  0.0 274.3 jit_solution(12656254474010272822)
XLA Ops:
  7.2 0.0 all-gather.4.cloned.1.call-start
  7.2 1.0 convert_reduce_fusion
  8.2 1.0 fusion.2
  9.2 9.9 %all_gather.16 = bf16[128,2048]{1,0:T(8,128)(2,1)S(1)} all-gather(bf16[128,1024]{1,0:T(8,128)(2,1)S(1)} %fusion.2), channel_id=1, replica_groups=mesh['dp'=16,'tensor'=2] {'tensor'}, dimensions={1}, use_global_device_ids=true | all-gather | bytes 786432 | tf_op jit(solution)/shard_map/all_gather | solution.py:27
  19.2 0.3 fusion.6
  19.5 1.0 convert_reduce_fusion.1
  20.5 1.0 fusion.1
  21.5 8.2 %all_gather.15 = bf16[128,2048]{1,0:T(8,128)(2,1)S(1)} all-gather(bf16[128,1024]{1,0:T(8,128)(2,1)S(1)} %fusion.1), channel_id=1, replica_groups=mesh['dp'=16,'tensor'=2] {'tensor'}, dimensions={1}, use_global_device_ids=true | all-gather | bytes 786432 | tf_op jit(solution)/shard_map/all_gather | solution.py:26
  29.7 0.9 multiply_reduce_fusion
  30.6 32.2 %all-reduce = (f32[]{:T(128)}, f32[]{:T(128)}, f32[]{:T(128)}) all-reduce(f32[]{:T(128)} %get-tuple-element.11, f32[]{:T(128)} %get-tuple-element.10, f32[]{:T(128)} %get-tuple-element.9), channel_id=1, replica_groups=mesh['dp'=16,'tensor'=2] {'dp'}, use_global_device_ids=true, to_apply=%region_2.0 | all-reduce | flops 3 | bytes 24 | tf_op jit(solution)/shard_map/psum | solution.py:31
  65.5 1.1 fusion
  66.5 0.0 all-gather.4.cloned.1.call-update
  66.6 0.0 all-gather.8.cloned.1.call-start
  66.6 0.7 all-gather.8.cloned.1.call-update
  67.3 0.0 all-gather.6.cloned.1.call-start
  67.4 0.7 all-gather.6.cloned.1.call-update
  68.1 46.5 %all-gather.4.cloned.1.call-done = bf16[2048,1024]{1,0:T(8,128)(2,1)} async-done(((bf16[128,1024]{1,0:T(8,128)(2,1)}), bf16[2048,1024]{1,0:T(8,128)(2,1)}) %all-gather.4.cloned.1.call-update) | async-done | bytes 4194320 | tf_op jit(solution)/shard_map/all_gather | solution.py:42
  114.6 6.3 %copy.9 = bf16[2,1024,1024]{1,2,0:T(8,128)(2,1)} copy(bf16[2,1024,1024]{2,1,0:T(8,128)(2,1)} %bitcast.17) | data formatting | bytes 8388608 | tf_op jit(solution)/shard_map/all_to_all | solution.py:43
  120.8 5.8 %all-to-all-start = ((bf16[2,1024,1024]{1,2,0:T(8,128)(2,1)}), bf16[2,1024,1024]{1,2,0:T(8,128)(2,1)}, u32[]{:S(2)}, u32[]{:S(2)}) async-start(bf16[2,1024,1024]{1,2,0:T(8,128)(2,1)} %copy.9), calls=%async_computation | async-start | bytes 8388608 | tf_op jit(solution)/shard_map/all_to_all | solution.py:43
  127.3 73.7 %all-gather.8.cloned.1.call-done = bf16[896,2048]{1,0:T(8,128)(2,1)} async-done(((bf16[896,1024]{1,0:T(8,128)(2,1)}), bf16[896,2048]{1,0:T(8,128)(2,1)}) %all-gather.8.cloned.1.call-update) | async-done | bytes 3670032 | tf_op jit(solution)/shard_map/all_gather | solution.py:53
  201.0 9.7 %convolution_bitcast_fusion = f32[896,1024]{0,1:T(8,128)} fusion(bf16[2048,1024]{1,0:T(8,128)(2,1)} %all-gather.4.cloned.1.call-done, bf16[896,2048]{1,0:T(8,128)(2,1)} %all-gather.8.cloned.1.call-done), kind=kOutput, calls=%fused_computation | convolution fusion | flops 3758096384 | bytes 11534336 | tf_op jit(solution)/shard_map/dot_general | solution.py:52
  210.7 5.3 %copy.11 = f32[896,1024]{1,0:T(8,128)} copy(f32[896,1024]{0,1:T(8,128)} %convolution_bitcast_fusion) | data formatting | bytes 7340032
  216.0 40.4 %all-gather.6.cloned.1.call-done = bf16[896,2048]{1,0:T(8,128)(2,1)} async-done(((bf16[896,1024]{1,0:T(8,128)(2,1)}), bf16[896,2048]{1,0:T(8,128)(2,1)}) %all-gather.6.cloned.1.call-update) | async-done | bytes 3670032 | tf_op jit(solution)/shard_map/all_gather | solution.py:46
  256.4 0.0 all-to-all-done
  256.4 7.9 %convert_bitcast_fusion = bf16[896,1024]{0,1:T(8,128)(2,1)S(1)} fusion(bf16[1024,2048]{0,1:T(8,128)(2,1)} %bitcast.2, bf16[896,2048]{1,0:T(8,128)(2,1)} %all-gather.6.cloned.1.call-done), kind=kOutput, calls=%fused_computation.1 | convolution fusion | flops 3759013888 | bytes 9699328 | tf_op jit(solution)/shard_map/dot_general | solution.py:45
  264.2 2.4 copy.10
  (2 shorter events, 0.0 us)
Async XLA Ops:
  7.2 107.4 %all-gather.4.cloned.1.call-start = ((), (), s32[]{:S(2)}) async-start(), calls=%async_computation.1 | async-start | bytes 4456448 | tf_op jit(solution)/shard_map/all_gather | solution.py:42
  66.6 134.5 %all-gather.8.cloned.1.call-start = ((), (), s32[]{:S(2)}) async-start(), calls=%async_computation.3 | async-start | bytes 5505024 | tf_op jit(solution)/shard_map/all_gather | solution.py:53
  67.3 189.1 %all-gather.6.cloned.1.call-start = ((), (), s32[]{:S(2)}) async-start(), calls=%async_computation.2 | async-start | bytes 5505024 | tf_op jit(solution)/shard_map/all_gather | solution.py:46
  120.8 135.6 %all-to-all-start = ((bf16[2,1024,1024]{1,2,0:T(8,128)(2,1)}), bf16[2,1024,1024]{1,2,0:T(8,128)(2,1)}, u32[]{:S(2)}, u32[]{:S(2)}) async-start(bf16[2,1024,1024]{1,2,0:T(8,128)(2,1)} %copy.9), calls=%async_computation | async-start | bytes 8388608 | tf_op jit(solution)/shard_map/all_to_all | solution.py:43
Sparse Core Ops, SparseCore 0:
  66.7 47.8 all-gather.3
  116.1 84.8 all-gather.7
  202.6 53.7 all-gather.5
where the time goes:
time: 275 us; the launch traced here: 274 us
  waiting for transfers between devices  162 us (59%)
  blocking collectives  50.3 us (18%)
  matrix products  19.8 us (7%)
  between operations  18.3 us (7%)
  local copies, waits for them, and re-layouts  14 us (5%)
  starting transfers between devices  5.92 us (2%)
  other arithmetic  4.02 us (1%)
    all_gather x1, waiting for transfers between devices, local(): lax.all_gather(hidden, 'tensor', axis=1, tiled=True)  73.7 us
    all_gather x1, waiting for transfers between devices, local(): columns = lax.all_gather(grad, 'dp', axis=0, tiled=True)  46.5 us
    all_gather x1, waiting for transfers between devices, local(): lax.all_gather(down_weight, 'tensor', axis=1, tiled=True)  40.4 us
    psum x1, blocking collectives, local(): lax.psum((jnp.sum(gram_x * gram_x), jnp.sum(gram_y * gram_y), jnp.sum(gra...  32.2 us
    all_gather x1, blocking collectives, local(): lax.all_gather(centered_y, 'tensor', axis=1, tiled=True)  9.94 us
    dot_general x1, matrix products, local(): lax.dot_general(lax.all_gather(hidden, 'tensor', axis=1, tiled=True), par...  9.7 us
    all_gather x1, blocking collectives, local(): lax.all_gather(centered_x, 'tensor', axis=1, tiled=True)  8.17 us
    dot_general x1, matrix products, local(): lax.dot_general(lax.all_gather(down_weight, 'tensor', axis=1, tiled=True)...  7.85 us
  transfers between devices with their start and end apart: 4, of which 3 were waited for; matrix products, arithmetic and copies ran while one was open for 8% of the time, Pallas kernels for 0%

commit v1 on v0

--- a/solution.py
+++ b/solution.py
@@ -1,7 +1,14 @@
+import functools
+
 import jax
 import jax.numpy as jnp
 from jax import lax
+from jax.experimental import pallas as pl
+from jax.experimental.pallas import tpu as pltpu
 from jax.sharding import PartitionSpec as P
+
+MESH = pl.DeviceIdType.MESH
+HIDDEN_PIECES = 7
 
 
 def center_rows(values):
@@ -15,7 +22,209 @@
     )
 
 
-def local(acts, partner, hidden, down_weight):
+def gather_kernel(
+    n_dp, scale, acts_ref, partner_ref, hidden_ref, cols_ref, other_hidden_ref, cka_ref,
+    grams, stats, mine,
+    hid_send, hid_recv, gram_send, gram_recv, stat_send, stat_recv,
+    up_send, up_recv, down_send, down_recv, sib_send, sib_recv, own_sem,
+):
+    tokens = acts_ref.shape[0]
+    chips, blocks_half = n_dp // 2, n_dp // 2
+    side = chips // 2
+    dp, tensor = lax.axis_index("dp"), lax.axis_index("tensor")
+    chip, core = dp // 2, dp % 2
+    column = chip % 2
+    pos = (1 - column) * (chip // 2) + column * (chips - 1 - chip // 2)
+
+    def chip_at(place):
+        far = place // side
+        return (1 - far) * (2 * place) + far * (2 * (chips - 1 - place) + 1)
+
+    def device_at(offset):
+        return chip_at((pos + offset + chips) % chips) * 2 + core
+
+    def rows_of(block):
+        half = (block // blocks_half + tensor) % 2
+        return (half * blocks_half + block % blocks_half) * tokens
+
+    peer = (dp, 1 - tensor)
+    sibling = (dp + 1 - 2 * core, tensor)
+    above, below = (device_at(1), tensor), (device_at(-1), tensor)
+    rounds = []
+    bit = 1
+    while bit < n_dp:
+        rounds.append((dp + bit * (1 - 2 * ((dp // bit) % 2)), tensor))
+        bit *= 2
+
+    barrier = pltpu.get_barrier_semaphore()
+    partners = [peer, above, below] + rounds
+    for other in partners:
+        pl.semaphore_signal(barrier, inc=1, device_id=other, device_id_type=MESH)
+    pl.semaphore_wait(barrier, len(partners))
+
+    piece = hidden_ref.shape[0] // HIDDEN_PIECES
+
+    def send_hidden(i):
+        rows = pl.ds(i * piece, piece)
+        return pltpu.make_async_remote_copy(
+            src_ref=hidden_ref.at[rows], dst_ref=other_hidden_ref.at[rows],
+            send_sem=hid_send.at[i], recv_sem=hid_recv.at[i],
+            device_id=peer, device_id_type=MESH,
+        )
+
+    hidden_copies = [send_hidden(i) for i in range(HIDDEN_PIECES)]
+    hidden_copies[0].start()
+
+    centered_x = center_rows(acts_ref[...])
+    centered_y = center_rows(partner_ref[...])
+    grams[0, 0] = token_gram(centered_x)
+    grams[0, 1] = token_gram(centered_y)
+    gram_copy = pltpu.make_async_remote_copy(
+        src_ref=grams.at[0], dst_ref=grams.at[1], send_sem=gram_send, recv_sem=gram_recv,
+        device_id=peer, device_id_type=MESH,
+    )
+    gram_copy.start()
+    for copy in hidden_copies[1:]:
+        copy.start()
+    gram_copy.wait()
+    gram_x = grams[0, 0] + grams[1, 0]
+    gram_y = grams[0, 1] + grams[1, 1]
+
+    stats[0] = jnp.zeros_like(stats[0])
+    stats[0, 0:1] = jnp.sum(gram_x * gram_x, axis=0, keepdims=True)
+    stats[0, 1:2] = jnp.sum(gram_y * gram_y, axis=0, keepdims=True)
+    stats[0, 2:3] = jnp.sum(gram_x * gram_y, axis=0, keepdims=True)
+    for i, other in enumerate(rounds):
+        copy = pltpu.make_async_remote_copy(
+            src_ref=stats.at[2 * i], dst_ref=stats.at[2 * i + 1],
+            send_sem=stat_send.at[i], recv_sem=stat_recv.at[i],
+            device_id=other, device_id_type=MESH,
+        )
+        copy.start()
+        copy.wait()
+        stats[2 * i + 2] = stats[2 * i] + stats[2 * i + 1]
+    sums = jnp.sum(stats[2 * len(rounds)], axis=1, keepdims=True)
+    sxx, syy, sxy = sums[0:1], sums[1:2], sums[2:3]
+    root = jnp.sqrt(sxx * syy)
+    cka_ref[...] = jnp.broadcast_to(sxy / root, cka_ref.shape)
+    ratio = sxy / sxx
+    coef = -2.0 * scale / root
+    mixed = gram_y - ratio * gram_x
+    grad = jnp.zeros(mine.shape, jnp.float32)
+    rest = mixed
+    for _ in range(3):
+        top = rest.astype(jnp.bfloat16)
+        rest = rest - top.astype(jnp.float32)
+        grad += jnp.dot(top, centered_x, preferred_element_type=jnp.float32)
+    mine[...] = (coef * grad).astype(jnp.bfloat16)
+
+    own_rows = pl.ds(pl.multiple_of(rows_of(dp), tokens), tokens)
+    own_copy = pltpu.make_async_copy(mine, cols_ref.at[own_rows], own_sem)
+    own_copy.start()
+
+    last = chips // 2
+
+    def ring(step, way):
+        block = device_at(-way * (step - 1))
+        start, size = rows_of(block), tokens
+        if step == last:
+            size = tokens // 2
+            start = start + (0 if way > 0 else size)
+        rows = pl.ds(pl.multiple_of(start, size), size)
+        sends, recvs = (up_send, up_recv) if way > 0 else (down_send, down_recv)
+        return pltpu.make_async_remote_copy(
+            src_ref=mine if step == 1 else cols_ref.at[rows], dst_ref=cols_ref.at[rows],
+            send_sem=sends.at[step - 1], recv_sem=recvs.at[step - 1],
+            device_id=above if way > 0 else below, device_id_type=MESH,
+        )
+
+    def share(i, block):
+        rows = pl.ds(pl.multiple_of(rows_of(block), tokens), tokens)
+        return pltpu.make_async_remote_copy(
+            src_ref=mine if i == 0 else cols_ref.at[rows], dst_ref=cols_ref.at[rows],
+            send_sem=sib_send.at[i], recv_sem=sib_recv.at[i],
+            device_id=sibling, device_id_type=MESH,
+        )
+
+    ups = [ring(step, 1) for step in range(1, last + 1)]
+    downs = [ring(step, -1) for step in range(1, last + 1)]
+    ups[0].start()
+    downs[0].start()
+    shares = [share(0, dp)]
+    shares[0].start()
+    for step in range(1, last):
+        for way, copies in ((1, ups), (-1, downs)):
+            copies[step - 1].wait_recv()
+            copies[step].start()
+            shares.append(share(len(shares), device_at(-way * step)))
+            shares[-1].start()
+    ups[-1].wait_recv()
+    downs[-1].wait_recv()
+    shares.append(share(len(shares), device_at(last)))
+    shares[-1].start()
+
+    own_copy.wait()
+    for copy in ups + downs:
+        copy.wait_send()
+    for copy in shares:
+        copy.wait()
+    for copy in hidden_copies:
+        copy.wait()
+
+
+def gather(acts, partner, hidden, scale):
+    n_dp = lax.axis_size("dp")
+    tokens, width = acts.shape
+    rounds = n_dp.bit_length() - 1
+    steps = n_dp // 4
+    dma = pltpu.SemaphoreType.DMA
+    vmem, anywhere = pl.BlockSpec(memory_space=pltpu.VMEM), pl.BlockSpec(memory_space=pl.ANY)
+    return pl.pallas_call(
+        functools.partial(gather_kernel, n_dp, scale),
+        out_shape=(
+            jax.ShapeDtypeStruct((n_dp * tokens, width), jnp.bfloat16),
+            jax.ShapeDtypeStruct(hidden.shape, jnp.bfloat16),
+            jax.ShapeDtypeStruct((8, 128), jnp.float32),
+        ),
+        in_specs=[vmem, vmem, anywhere],
+        out_specs=(anywhere, anywhere, vmem),
+        scratch_shapes=[
+            pltpu.VMEM((2, 2, tokens, tokens), jnp.float32),
+            pltpu.VMEM((2 * rounds + 1, 8, tokens), jnp.float32),
+            pltpu.VMEM((tokens, width), jnp.bfloat16),
+            dma((HIDDEN_PIECES,)), dma((HIDDEN_PIECES,)), dma, dma,
+            dma((rounds,)), dma((rounds,)),
+            dma((steps,)), dma((steps,)), dma((steps,)), dma((steps,)),
+            dma((2 * steps,)), dma((2 * steps,)), dma,
+        ],
+        compiler_params=pltpu.CompilerParams(
+            collective_id=0, has_side_effects=True, vmem_limit_bytes=32 * 2**20
+        ),
+    )(acts, partner, hidden)
+
+
+def paired(acts, partner, hidden, down_weight):
+    tokens = acts.shape[0]
+    width = acts.shape[1] * lax.axis_size("tensor")
+    scale = float(tokens * lax.axis_size("dp") * width)
+    cols, other_hidden, cka = gather(acts, partner, hidden, scale)
+    half = cols.shape[0] // 2
+    own, other = cols[:half], cols[half:]
+    contract = (((1,), (1,)), ((), ()))
+    theirs = lax.dot_general(
+        down_weight, other, contract, preferred_element_type=jnp.float32
+    ).astype(jnp.bfloat16)
+    arrived = lax.ppermute(theirs, "tensor", [(0, 1), (1, 0)])
+    ours = lax.dot_general(down_weight, own, contract, preferred_element_type=jnp.float32)
+    grad_weight = jnp.dot(hidden, own, preferred_element_type=jnp.float32) + jnp.dot(
+        other_hidden, other, preferred_element_type=jnp.float32
+    )
+    ours, grad_weight, arrived = lax.optimization_barrier((ours, grad_weight, arrived))
+    grad_hidden = (ours + arrived.astype(jnp.float32)).astype(jnp.bfloat16)
+    return (grad_hidden, grad_weight, cka[0, 0])
+
+
+def gathered(acts, partner, hidden, down_weight):
     rows = acts.shape[0]
     width = acts.shape[1] * lax.axis_size("tensor")
     total = rows * lax.axis_size("dp")
@@ -41,17 +250,15 @@
     ).astype(jnp.bfloat16)
     columns = lax.all_gather(grad, "dp", axis=0, tiled=True)
     token_block = lax.all_to_all(columns, "tensor", split_axis=0, concat_axis=1, tiled=True)
-    part_grad = token_block
     grad_hidden = lax.dot_general(
         lax.all_gather(down_weight, "tensor", axis=1, tiled=True),
-        part_grad,
+        token_block,
         (((1,), (1,)), ((), ())),
         preferred_element_type=jnp.float32,
     ).astype(jnp.bfloat16)
-    part_grad = columns
     grad_weight = lax.dot_general(
         lax.all_gather(hidden, "tensor", axis=1, tiled=True),
-        part_grad,
+        columns,
         (((1,), (0,)), ((), ())),
         preferred_element_type=jnp.float32,
     )
@@ -59,6 +266,10 @@
 
 
 def solution(mesh):
-    in_specs = (P("dp", "tensor"), P("dp", "tensor"), P("dp", "tensor"), P("dp", "tensor"))
-    out_specs = (P("dp", "tensor"), P("dp", "tensor"), P())
-    return jax.shard_map(local, mesh=mesh, in_specs=in_specs, out_specs=out_specs, check_vma=False)
+    n_dp, n_tensor = mesh.shape["dp"], mesh.shape["tensor"]
+    fits = n_tensor == 2 and n_dp >= 8 and n_dp & (n_dp - 1) == 0
+    spec = P("dp", "tensor")
+    return jax.shard_map(
+        paired if fits else gathered,
+        mesh=mesh, in_specs=(spec,) * 4, out_specs=(spec, spec, P()), check_vma=False,
+    )

time: 275 us -> 112 us (0.41)
  waiting for transfers between devices: 162 us -> 32 us
  Pallas kernels: 0 us -> 52 us
  blocking collectives: 50.3 us -> 0 us
  between operations: 18.3 us -> 0.69 us
  matrix products: 19.8 us -> 11.4 us
  starting transfers between devices: 5.92 us -> 0.78 us
    all_gather x3 -> x0, waiting for transfers between devices: 161 us -> none  [the longest x1 73.7 us: local(): lax.all_gather(hidden, 'tensor', axis=1, tiled=True)]
    pallas_call x0 -> x1, Pallas kernels: none -> 52 us  [gather(): pl.pallas_call(functools.partial(gather_kernel, n_dp, scale), out_shape=(...]
    psum x1 -> x0, blocking collectives: 32.2 us -> none  [local(): lax.psum((jnp.sum(gram_x * gram_x), jnp.sum(gram_y * gram_y), jnp.sum(gra...]
    ppermute x0 -> x1, waiting for transfers between devices: none -> 32 us  [paired(): arrived = lax.ppermute(theirs, 'tensor', [(0, 1), (1, 0)])]
    all_gather x2 -> x0, blocking collectives: 18.1 us -> none  [the longest x1 9.94 us: local(): lax.all_gather(centered_y, 'tensor', axis=1, tiled=True)]
    dot_general x5 -> x4, matrix products: 19.8 us -> 11.4 us  [the longest x1 4.22 us: paired(): jnp.dot(hidden, own, preferred_element_type=jnp.float32)]
    all_to_all x1 -> x0, local copies, waits for them, and re-layouts: 6.27 us -> none  [local(): lax.all_to_all(columns, 'tensor', split_axis=0, concat_axis=1, tiled=True)]
    all_to_all x1 -> x0, starting transfers between devices: 5.8 us -> none  [local(): lax.all_to_all(columns, 'tensor', split_axis=0, concat_axis=1, tiled=True)]
  transfers between devices with their start and end apart: 4 -> 1, of which waited for: 3 -> 1; matrix products, arithmetic and copies ran while one was open for 8% -> 9% of each run, Pallas kernels for 0% -> 0%
where the time goes in v1:
time: 112 us; the launch traced here: 111 us
  Pallas kernels  52 us (46%)
  waiting for transfers between devices  32 us (29%)
  local copies, waits for them, and re-layouts  12.8 us (11%)
  matrix products  11.4 us (10%)
  other arithmetic  1.57 us (1%)
    pallas_call x1, Pallas kernels, gather(): pl.pallas_call(functools.partial(gather_kernel, n_dp, scale), out_shape=(...  52 us
    ppermute x1, waiting for transfers between devices, paired(): arrived = lax.ppermute(theirs, 'tensor', [(0, 1), (1, 0)])  32 us
    unnamed x10, local copies, waits for them, and re-layouts  12.3 us
    dot_general x1, matrix products, paired(): jnp.dot(hidden, own, preferred_element_type=jnp.float32)  4.22 us
    dot_general x1, matrix products, paired(): jnp.dot(other_hidden, other, preferred_element_type=jnp.float32)  2.44 us
    dot_general x1, matrix products, paired(): lax.dot_general(down_weight, other, contract, preferred_element_type=jnp....  2.37 us
    dot_general x1, matrix products, paired(): lax.dot_general(down_weight, own, contract, preferred_element_type=jnp.fl...  2.37 us
  transfers between devices with their start and end apart: 1, of which 1 were waited for; matrix products, arithmetic and copies ran while one was open for 9% of the time, Pallas kernels for 0%

profile of v1, /device:TPU:0, one launch (start us, length us, event | category | flops | bytes accessed | tf_op | source)
XLA Modules:
  0.0 111.2 jit_solution(3882478159291011131)
XLA Ops:
  0.6 0.0 copy-start
  0.6 0.0 copy-start.1
  0.7 1.6 %copy-done.1 = bf16[896,1024]{1,0:T(8,128)(2,1)S(1)} copy-done((bf16[896,1024]{1,0:T(8,128)(2,1)S(1)}, bf16[896,1024]{1,0:T(8,128)(2,1)}, u32[]{:S(2)}) %copy-start.1) | copy-done | bytes 1835032
  2.3 0.0 copy-start.2
  2.3 0.9 copy-done.2
  3.2 0.0 copy-start.3
  3.2 0.9 copy-done.3
  4.2 52.0 %shard_map.67 = (bf16[2048,1024]{1,0:T(8,128)(2,1)S(1)}, bf16[896,1024]{1,0:T(8,128)(2,1)S(1)}, f32[8,128]{1,0:T(8,128)S(1)}) custom-call(bf16[128,1024]{1,0:T(8,128)(2,1)S(1)} %copy-done.2, bf16[128,1024]{1,0:T(8,128)(2,1)S(1)} %copy-done.3, bf16[896,1024]{1,0:T(8,128)(2,1)S(1)} %copy-done.1), custom_call_target="tpu_custom_call" | custom-call | tf_op jit(solution)/shard_map/pallas_call | solution.py:182
  56.2 0.0 copy-done
  56.2 2.4 %convert_bitcast_fusion = bf16[896,1024]{0,1:T(8,128)(2,1)S(1)} fusion(bf16[896,1024]{1,0:T(8,128)(2,1)S(1)} %copy-done, bf16[2048,1024]{1,0:T(8,128)(2,1)S(1)} %get-tuple-element.9), kind=kOutput, calls=%fused_computation.9 | convolution fusion | flops 1879965696 | bytes 5767168 | tf_op jit(solution)/shard_map/dot_general | solution.py:214
  58.6 0.8 collective-permute-start
  59.3 0.5 slice.11
  59.9 2.4 %convolution_bitcast_fusion = f32[896,1024]{0,1:T(8,128)S(1)} fusion(bf16[896,1024]{1,0:T(8,128)(2,1)S(1)} %copy-done, bf16[2048,1024]{1,0:T(8,128)(2,1)S(1)} %get-tuple-element.9), kind=kOutput, calls=%fused_computation.2 | convolution fusion | flops 1879048192 | bytes 7602176 | tf_op jit(solution)/shard_map/dot_general | solution.py:218
  62.2 2.4 %fusion.2 = f32[896,1024]{0,1:T(8,128)S(1)} fusion(bf16[896,1024]{1,0:T(8,128)(2,1)S(1)} %get-tuple-element.10, bf16[2048,1024]{1,0:T(8,128)(2,1)S(1)} %get-tuple-element.9), kind=kOutput, calls=%fused_computation.5 | convolution fusion | flops 1879048192 | bytes 7602176 | tf_op jit(solution)/shard_map/dot_general | solution.py:219
  64.7 4.2 %bitcast_add_fusion = f32[896,1024]{0,1:T(8,128)} fusion(f32[896,1024]{0,1:T(8,128)S(1)} %fusion.2, bf16[896,1024]{1,0:T(8,128)(2,1)S(1)} %copy-done.1, bf16[2048,1024]{1,0:T(8,128)(2,1)S(1)} %get-tuple-element.9), kind=kOutput, calls=%fused_computation | convolution fusion | flops 1879965696 | bytes 11272192 | tf_op jit(solution)/shard_map/dot_general | solution.py:219
  68.9 32.0 %collective-permute-done = bf16[896,1024]{0,1:T(8,128)(2,1)S(1)} collective-permute-done((bf16[896,1024]{0,1:T(8,128)(2,1)S(1)}, bf16[896,1024]{0,1:T(8,128)(2,1)S(1)}, u32[]{:S(2)}, u32[]{:S(2)}) %collective-permute-start) | collective-permute-done | bytes 1835040 | tf_op jit(solution)/shard_map/ppermute | solution.py:217
  100.9 1.6 %add_convert_fusion = bf16[896,1024]{0,1:T(8,128)(2,1)} fusion(f32[896,1024]{0,1:T(8,128)S(1)} %convolution_bitcast_fusion, bf16[896,1024]{0,1:T(8,128)(2,1)S(1)} %collective-permute-done), kind=kLoop, calls=%fused_computation.1 | loop fusion | flops 2752512 | bytes 7340032 | tf_op jit(solution)/shard_map/convert_element_type | solution.py:223
  102.5 3.8 %copy.8 = bf16[896,1024]{1,0:T(8,128)(2,1)} copy(bf16[896,1024]{0,1:T(8,128)(2,1)} %add_convert_fusion) | data formatting | bytes 3670016
  106.3 5.0 %copy.9 = f32[896,1024]{1,0:T(8,128)} copy(f32[896,1024]{0,1:T(8,128)} %bitcast_add_fusion) | data formatting | bytes 7340032
Async XLA Ops:
  0.6 55.5 %copy-start = (bf16[896,1024]{1,0:T(8,128)(2,1)S(1)}, bf16[896,1024]{1,0:T(8,128)(2,1)}, u32[]{:S(2)}) copy-start(bf16[896,1024]{1,0:T(8,128)(2,1)} %param.7) | copy-start | bytes 5505028
  0.6 1.6 %copy-start.1 = (bf16[896,1024]{1,0:T(8,128)(2,1)S(1)}, bf16[896,1024]{1,0:T(8,128)(2,1)}, u32[]{:S(2)}) copy-start(bf16[896,1024]{1,0:T(8,128)(2,1)} %hidden_ref.1) | copy-start | bytes 5505028
  2.3 0.9 copy-start.2
  3.2 0.9 copy-start.3
  58.6 42.4 %collective-permute-start = (bf16[896,1024]{0,1:T(8,128)(2,1)S(1)}, bf16[896,1024]{0,1:T(8,128)(2,1)S(1)}, u32[]{:S(2)}, u32[]{:S(2)}) collective-permute-start(bf16[896,1024]{0,1:T(8,128)(2,1)S(1)} %convert_bitcast_fusion), channel_id=1, source_target_pairs={{0,1},{1,0},{2,3},{3,2},{4,5},{5,4},{6,7},{7,6},{8,9},{9,8},{10,11... | collective-permute-start | bytes 5505032 | tf_op jit(solution)/shard_map/ppermute | solution.py:217

commit v2 on v1

--- a/solution.py
+++ b/solution.py
@@ -8,7 +8,7 @@
 from jax.sharding import PartitionSpec as P
 
 MESH = pl.DeviceIdType.MESH
-HIDDEN_PIECES = 7
+TILE = 256
 
 
 def center_rows(values):
@@ -23,9 +23,9 @@
 
 
 def gather_kernel(
-    n_dp, scale, acts_ref, partner_ref, hidden_ref, cols_ref, other_hidden_ref, cka_ref,
+    n_dp, scale, acts_ref, partner_ref, cols_ref, cka_ref,
     grams, stats, mine,
-    hid_send, hid_recv, gram_send, gram_recv, stat_send, stat_recv,
+    gram_send, gram_recv, stat_send, stat_recv,
     up_send, up_recv, down_send, down_recv, sib_send, sib_recv, own_sem,
 ):
     tokens = acts_ref.shape[0]
@@ -62,19 +62,6 @@
         pl.semaphore_signal(barrier, inc=1, device_id=other, device_id_type=MESH)
     pl.semaphore_wait(barrier, len(partners))
 
-    piece = hidden_ref.shape[0] // HIDDEN_PIECES
-
-    def send_hidden(i):
-        rows = pl.ds(i * piece, piece)
-        return pltpu.make_async_remote_copy(
-            src_ref=hidden_ref.at[rows], dst_ref=other_hidden_ref.at[rows],
-            send_sem=hid_send.at[i], recv_sem=hid_recv.at[i],
-            device_id=peer, device_id_type=MESH,
-        )
-
-    hidden_copies = [send_hidden(i) for i in range(HIDDEN_PIECES)]
-    hidden_copies[0].start()
-
     centered_x = center_rows(acts_ref[...])
     centered_y = center_rows(partner_ref[...])
     grams[0, 0] = token_gram(centered_x)
@@ -84,8 +71,6 @@
         device_id=peer, device_id_type=MESH,
     )
     gram_copy.start()
-    for copy in hidden_copies[1:]:
-        copy.start()
     gram_copy.wait()
     gram_x = grams[0, 0] + grams[1, 0]
     gram_y = grams[0, 1] + grams[1, 1]
@@ -168,11 +153,9 @@
         copy.wait_send()
     for copy in shares:
         copy.wait()
-    for copy in hidden_copies:
-        copy.wait()
-
-
-def gather(acts, partner, hidden, scale):
+
+
+def gather(acts, partner, scale):
     n_dp = lax.axis_size("dp")
     tokens, width = acts.shape
     rounds = n_dp.bit_length() - 1
@@ -183,16 +166,15 @@
         functools.partial(gather_kernel, n_dp, scale),
         out_shape=(
             jax.ShapeDtypeStruct((n_dp * tokens, width), jnp.bfloat16),
-            jax.ShapeDtypeStruct(hidden.shape, jnp.bfloat16),
             jax.ShapeDtypeStruct((8, 128), jnp.float32),
         ),
-        in_specs=[vmem, vmem, anywhere],
-        out_specs=(anywhere, anywhere, vmem),
+        in_specs=[vmem, vmem],
+        out_specs=(anywhere, vmem),
         scratch_shapes=[
             pltpu.VMEM((2, 2, tokens, tokens), jnp.float32),
             pltpu.VMEM((2 * rounds + 1, 8, tokens), jnp.float32),
             pltpu.VMEM((tokens, width), jnp.bfloat16),
-            dma((HIDDEN_PIECES,)), dma((HIDDEN_PIECES,)), dma, dma,
+            dma, dma,
             dma((rounds,)), dma((rounds,)),
             dma((steps,)), dma((steps,)), dma((steps,)), dma((steps,)),
             dma((2 * steps,)), dma((2 * steps,)), dma,
@@ -200,26 +182,81 @@
         compiler_params=pltpu.CompilerParams(
             collective_id=0, has_side_effects=True, vmem_limit_bytes=32 * 2**20
         ),
-    )(acts, partner, hidden)
+        cost_estimate=pl.CostEstimate(
+            flops=8 * tokens * tokens * width, transcendentals=0,
+            bytes_accessed=80 * n_dp * tokens * width,
+        ),
+    )(acts, partner)
+
+
+def by_tokens_kernel(weight_ref, grad_ref, out_ref):
+    out_ref[...] = lax.dot_general(
+        weight_ref[...], grad_ref[...], (((1,), (1,)), ((), ())), preferred_element_type=jnp.float32
+    ).astype(out_ref.dtype)
+
+
+def by_tokens(weight, cols, half, dtype):
+    rows, width = weight.shape
+    tokens = cols.shape[0] // 2
+    tile = min(TILE, tokens)
+    steps = tokens // tile
+    return pl.pallas_call(
+        by_tokens_kernel,
+        grid=(steps,),
+        out_shape=jax.ShapeDtypeStruct((rows, tokens), dtype),
+        in_specs=[
+            pl.BlockSpec((rows, width), lambda i: (0, 0)),
+            pl.BlockSpec((tile, width), lambda i: (half * steps + i, 0)),
+        ],
+        out_specs=pl.BlockSpec((rows, tile), lambda i: (0, i)),
+        compiler_params=pltpu.CompilerParams(vmem_limit_bytes=32 * 2**20),
+        cost_estimate=pl.CostEstimate(
+            flops=2 * rows * tokens * width, transcendentals=0,
+            bytes_accessed=2 * (rows * width + tokens * width + 2 * rows * tokens),
+        ),
+    )(weight, cols)
+
+
+def over_tokens_kernel(own_ref, other_ref, grad_own_ref, grad_other_ref, out_ref):
+    out_ref[...] = jnp.dot(
+        own_ref[...], grad_own_ref[...], preferred_element_type=jnp.float32
+    ) + jnp.dot(other_ref[...], grad_other_ref[...], preferred_element_type=jnp.float32)
+
+
+def over_tokens(own, other, cols):
+    rows, tokens = own.shape
+    width = cols.shape[1]
+    tile = min(TILE, width)
+    whole = pl.BlockSpec((rows, tokens), lambda i: (0, 0))
+    return pl.pallas_call(
+        over_tokens_kernel,
+        grid=(width // tile,),
+        out_shape=jax.ShapeDtypeStruct((rows, width), jnp.float32),
+        in_specs=[
+            whole, whole,
+            pl.BlockSpec((tokens, tile), lambda i: (0, i)),
+            pl.BlockSpec((tokens, tile), lambda i: (1, i)),
+        ],
+        out_specs=pl.BlockSpec((rows, tile), lambda i: (0, i)),
+        compiler_params=pltpu.CompilerParams(vmem_limit_bytes=32 * 2**20),
+        cost_estimate=pl.CostEstimate(
+            flops=4 * rows * tokens * width, transcendentals=0,
+            bytes_accessed=4 * (rows * tokens + tokens * width + rows * width),
+        ),
+    )(own, other, cols, cols)
 
 
 def paired(acts, partner, hidden, down_weight):
     tokens = acts.shape[0]
     width = acts.shape[1] * lax.axis_size("tensor")
     scale = float(tokens * lax.axis_size("dp") * width)
-    cols, other_hidden, cka = gather(acts, partner, hidden, scale)
-    half = cols.shape[0] // 2
-    own, other = cols[:half], cols[half:]
-    contract = (((1,), (1,)), ((), ()))
-    theirs = lax.dot_general(
-        down_weight, other, contract, preferred_element_type=jnp.float32
-    ).astype(jnp.bfloat16)
-    arrived = lax.ppermute(theirs, "tensor", [(0, 1), (1, 0)])
-    ours = lax.dot_general(down_weight, own, contract, preferred_element_type=jnp.float32)
-    grad_weight = jnp.dot(hidden, own, preferred_element_type=jnp.float32) + jnp.dot(
-        other_hidden, other, preferred_element_type=jnp.float32
-    )
-    ours, grad_weight, arrived = lax.optimization_barrier((ours, grad_weight, arrived))
+    swap = [(0, 1), (1, 0)]
+    other_hidden = lax.ppermute(hidden, "tensor", swap)
+    cols, cka = gather(acts, partner, scale)
+    theirs = by_tokens(down_weight, cols, 1, jnp.bfloat16)
+    arrived = lax.ppermute(theirs, "tensor", swap)
+    ours = by_tokens(down_weight, cols, 0, jnp.float32)
+    grad_weight = over_tokens(hidden, other_hidden, cols)
     grad_hidden = (ours + arrived.astype(jnp.float32)).astype(jnp.bfloat16)
     return (grad_hidden, grad_weight, cka[0, 0])
 

time: 112 us -> 135 us (1.21)
  Pallas kernels: 52 us -> 92.4 us
  matrix products: 11.4 us -> 0 us
  local copies, waits for them, and re-layouts: 12.8 us -> 3.91 us
  starting transfers between devices: 0.78 us -> 4.63 us
    pallas_call x1, Pallas kernels: 52 us -> 80.5 us  [gather(): pl.pallas_call(functools.partial(gather_kernel, n_dp, scale), out_shape=(...]
    pallas_call x0 -> x3, Pallas kernels: none -> 11.9 us  [the longest x1 6.02 us: over_tokens(): pl.pallas_call(over_tokens_kernel, grid=(width // tile,), out_shape=jax.S...]
    dot_general x4 -> x0, matrix products: 11.4 us -> none  [the longest x1 4.22 us: paired(): jnp.dot(hidden, own, preferred_element_type=jnp.float32)]
    unnamed x10 -> x8, local copies, waits for them, and re-layouts: 12.3 us -> 3.4 us
    ppermute x1 -> x2, starting transfers between devices: 0.78 us -> 4.63 us  [the longest x1 3.03 us: paired(): other_hidden = lax.ppermute(hidden, 'tensor', swap)]
    ppermute x1 -> x2, waiting for transfers between devices: 32 us -> 31.2 us  [the longest x1 31.2 us: paired(): arrived = lax.ppermute(theirs, 'tensor', swap)]
  transfers between devices with their start and end apart: 1 -> 2, of which waited for: 1 -> 1; matrix products, arithmetic and copies ran while one was open for 9% -> 0% of each run, Pallas kernels for 0% -> 69%
where the time goes in v2:
time: 135 us
  Pallas kernels  92.4 us (68%)
  waiting for transfers between devices  31.2 us (23%)
  starting transfers between devices  4.63 us (3%)
  local copies, waits for them, and re-layouts  3.91 us (3%)
  other arithmetic  1.9 us (1%)
    pallas_call x1, Pallas kernels, gather(): pl.pallas_call(functools.partial(gather_kernel, n_dp, scale), out_shape=(...  80.5 us
    ppermute x1, waiting for transfers between devices, paired(): arrived = lax.ppermute(theirs, 'tensor', swap)  31.2 us
    pallas_call x1, Pallas kernels, over_tokens(): pl.pallas_call(over_tokens_kernel, grid=(width // tile,), out_shape=jax.S...  6.02 us
    pallas_call x2, Pallas kernels, by_tokens(): pl.pallas_call(by_tokens_kernel, grid=(steps,), out_shape=jax.ShapeDtypeS...  5.87 us
    unnamed x8, local copies, waits for them, and re-layouts  3.4 us
    ppermute x1, starting transfers between devices, paired(): other_hidden = lax.ppermute(hidden, 'tensor', swap)  3.03 us
  transfers between devices with their start and end apart: 2, of which 1 were waited for; matrix products, arithmetic and copies ran while one was open for 0% of the time, Pallas kernels for 69%

profile of v2, /device:TPU:0, one launch (start us, length us, event | category | flops | bytes accessed | tf_op | source)
XLA Modules:
  0.0 134.7 jit_solution(11731781584614670230)
XLA Ops:
  0.6 3.0 %collective-permute-start.1 = (bf16[896,1024]{1,0:T(8,128)(2,1)}, bf16[896,1024]{1,0:T(8,128)(2,1)S(1)}, u32[]{:S(2)}, u32[]{:S(2)}) collective-permute-start(bf16[896,1024]{1,0:T(8,128)(2,1)} %own_ref.1), channel_id=1, source_target_pairs={{0,1},{1,0},{2,3},{3,2},{4,5},{5,4},{6,7},{7,6},{8,9},{9,8},{10,11... | collective-permute-start | bytes 5505032 | tf_op jit(solution)/shard_map/ppermute | solution.py:254
  3.7 0.0 copy-start.2
  3.7 0.9 copy-done.2
  4.6 0.0 copy-start.3
  4.6 0.9 copy-done.3
  5.6 80.5 %shard_map.67 = (bf16[2048,1024]{1,0:T(8,128)(2,1)S(1)}, f32[8,128]{1,0:T(8,128)S(1)}) custom-call(bf16[128,1024]{1,0:T(8,128)(2,1)S(1)} %copy-done.2, bf16[128,1024]{1,0:T(8,128)(2,1)S(1)} %copy-done.3), custom_call_target="tpu_custom_call" | custom-call | flops 134217728 | bytes 167772160 | tf_op jit(solution)/shard_map/pallas_call | solution.py:165
  86.0 0.0 copy-start
  86.1 1.5 %copy-done = bf16[896,1024]{1,0:T(8,128)(2,1)S(1)} copy-done((bf16[896,1024]{1,0:T(8,128)(2,1)S(1)}, bf16[896,1024]{1,0:T(8,128)(2,1)}, u32[]{:S(2)}) %copy-start) | copy-done | bytes 1835032
  87.5 2.9 %shard_map.69 = bf16[896,1024]{1,0:T(8,128)(2,1)S(1)} custom-call(bf16[896,1024]{1,0:T(8,128)(2,1)S(1)} %copy-done, bf16[2048,1024]{1,0:T(8,128)(2,1)S(1)} %get-tuple-element.5.grad_ref.grad_own_ref.grad_other_ref), custom_call_target="tpu_custom_call" | custom-call | flops 1879048192 | bytes 7602176 | tf_op jit(solution)/shard_map/pallas_call | solution.py:203
  90.5 1.6 %collective-permute-start = (bf16[896,1024]{1,0:T(8,128)(2,1)S(1)}, bf16[896,1024]{1,0:T(8,128)(2,1)S(1)}, u32[]{:S(2)}, u32[]{:S(2)}) collective-permute-start(bf16[896,1024]{1,0:T(8,128)(2,1)S(1)} %shard_map.69), channel_id=1, source_target_pairs={{0,1},{1,0},{2,3},{3,2},{4,5},{5,4},{6,7},{7,6},{8,9},{9,8},{10,11... | collective-permute-start | bytes 5505032 | tf_op jit(solution)/shard_map/ppermute | solution.py:257
  92.1 0.5 slice.3
  92.6 0.0 copy-start.1
  92.6 3.0 %shard_map.68 = f32[896,1024]{1,0:T(8,128)S(1)} custom-call(bf16[896,1024]{1,0:T(8,128)(2,1)S(1)} %copy-done, bf16[2048,1024]{1,0:T(8,128)(2,1)S(1)} %get-tuple-element.5.grad_ref.grad_own_ref.grad_other_ref), custom_call_target="tpu_custom_call" | custom-call | flops 1879048192 | bytes 7602176 | tf_op jit(solution)/shard_map/pallas_call | solution.py:203
  95.5 0.0 collective-permute-done.1.other_ref
  95.5 0.0 copy-done.1
  95.6 6.0 %shard_map.70 = f32[896,1024]{1,0:T(8,128)} custom-call(bf16[896,1024]{1,0:T(8,128)(2,1)S(1)} %copy-done.1, bf16[896,1024]{1,0:T(8,128)(2,1)S(1)} %collective-permute-done.1.other_ref, bf16[2048,1024]{1,0:T(8,128)(2,1)S(1)} %get-tuple-element.5.grad_ref.grad_own_ref.grad_other_ref, bf16[2048,1024]{1,0:T(8,128)(2,1)S(1)} %get-tuple-element.5.grad_ref.grad_own_ref.grad_other_ref), custom_call_target="tpu_custom_call" | custom-call | flops 3758096384 | bytes 11534336 | tf_op jit(solution)/shard_map/pallas_call | solution.py:231
  101.6 31.2 %collective-permute-done = bf16[896,1024]{1,0:T(8,128)(2,1)S(1)} collective-permute-done((bf16[896,1024]{1,0:T(8,128)(2,1)S(1)}, bf16[896,1024]{1,0:T(8,128)(2,1)S(1)}, u32[]{:S(2)}, u32[]{:S(2)}) %collective-permute-start) | collective-permute-done | bytes 1835040 | tf_op jit(solution)/shard_map/ppermute | solution.py:257
  132.8 1.9 %add_convert_fusion = bf16[896,1024]{1,0:T(8,128)(2,1)} fusion(f32[896,1024]{1,0:T(8,128)S(1)} %shard_map.68, bf16[896,1024]{1,0:T(8,128)(2,1)S(1)} %collective-permute-done), kind=kLoop, calls=%fused_computation | loop fusion | flops 2752512 | bytes 7340032 | tf_op jit(solution)/shard_map/convert_element_type | solution.py:260
Async XLA Ops:
  0.6 94.9 %collective-permute-start.1 = (bf16[896,1024]{1,0:T(8,128)(2,1)}, bf16[896,1024]{1,0:T(8,128)(2,1)S(1)}, u32[]{:S(2)}, u32[]{:S(2)}) collective-permute-start(bf16[896,1024]{1,0:T(8,128)(2,1)} %own_ref.1), channel_id=1, source_target_pairs={{0,1},{1,0},{2,3},{3,2},{4,5},{5,4},{6,7},{7,6},{8,9},{9,8},{10,11... | collective-permute-start | bytes 5505032 | tf_op jit(solution)/shard_map/ppermute | solution.py:254
  3.7 0.9 copy-start.2
  4.6 0.9 copy-start.3
  86.0 1.5 %copy-start = (bf16[896,1024]{1,0:T(8,128)(2,1)S(1)}, bf16[896,1024]{1,0:T(8,128)(2,1)}, u32[]{:S(2)}) copy-start(bf16[896,1024]{1,0:T(8,128)(2,1)} %weight_ref.3) | copy-start | bytes 5505028
  90.5 42.3 %collective-permute-start = (bf16[896,1024]{1,0:T(8,128)(2,1)S(1)}, bf16[896,1024]{1,0:T(8,128)(2,1)S(1)}, u32[]{:S(2)}, u32[]{:S(2)}) collective-permute-start(bf16[896,1024]{1,0:T(8,128)(2,1)S(1)} %shard_map.69), channel_id=1, source_target_pairs={{0,1},{1,0},{2,3},{3,2},{4,5},{5,4},{6,7},{7,6},{8,9},{9,8},{10,11... | collective-permute-start | bytes 5505032 | tf_op jit(solution)/shard_map/ppermute | solution.py:257
  92.6 3.0 %copy-start.1 = (bf16[896,1024]{1,0:T(8,128)(2,1)S(1)}, bf16[896,1024]{1,0:T(8,128)(2,1)}, u32[]{:S(2)}) copy-start(bf16[896,1024]{1,0:T(8,128)(2,1)} %own_ref.1) | copy-start | bytes 5505028

commit v3 on v1

--- a/solution.py
+++ b/solution.py
@@ -8,7 +8,9 @@
 from jax.sharding import PartitionSpec as P
 
 MESH = pl.DeviceIdType.MESH
-HIDDEN_PIECES = 7
+FIRST = 64
+PARTS = 4
+TILE = 256
 
 
 def center_rows(values):
@@ -22,13 +24,14 @@
     )
 
 
-def gather_kernel(
-    n_dp, scale, acts_ref, partner_ref, hidden_ref, cols_ref, other_hidden_ref, cka_ref,
-    grams, stats, mine,
-    hid_send, hid_recv, gram_send, gram_recv, stat_send, stat_recv,
-    up_send, up_recv, down_send, down_recv, sib_send, sib_recv, own_sem,
+def fused_kernel(
+    n_dp, scale, acts_hbm, partner_hbm, hidden_hbm, weight_hbm, grad_hidden_hbm, grad_weight_hbm, cka_ref,
+    acts, partner, hidden, weight, other_hidden, cols, theirs, arrived, ours, grad_hidden, grad_weight, grams, stats,
+    load_sem, weight_sem, store_sem, hid_send, hid_recv, gram_send, gram_recv, stat_send, stat_recv,
+    up_send, up_recv, down_send, down_recv, sib_send, sib_recv, part_send, part_recv,
 ):
-    tokens = acts_ref.shape[0]
+    tokens = acts.shape[0]
+    rows = hidden.shape[0]
     chips, blocks_half = n_dp // 2, n_dp // 2
     side = chips // 2
     dp, tensor = lax.axis_index("dp"), lax.axis_index("tensor")
@@ -46,6 +49,15 @@
     def rows_of(block):
         half = (block // blocks_half + tensor) % 2
         return (half * blocks_half + block % blocks_half) * tokens
+
+    loads = [
+        pltpu.make_async_copy(source, target, load_sem.at[i])
+        for i, (source, target) in enumerate(
+            ((acts_hbm, acts), (partner_hbm, partner), (hidden_hbm, hidden), (weight_hbm, weight))
+        )
+    ]
+    for load in loads:
+        load.start()
 
     peer = (dp, 1 - tensor)
     sibling = (dp + 1 - 2 * core, tensor)
@@ -62,21 +74,21 @@
         pl.semaphore_signal(barrier, inc=1, device_id=other, device_id_type=MESH)
     pl.semaphore_wait(barrier, len(partners))
 
-    piece = hidden_ref.shape[0] // HIDDEN_PIECES
-
-    def send_hidden(i):
-        rows = pl.ds(i * piece, piece)
+    def send_hidden(i, start, size):
+        part = pl.ds(start, size)
         return pltpu.make_async_remote_copy(
-            src_ref=hidden_ref.at[rows], dst_ref=other_hidden_ref.at[rows],
+            src_ref=hidden_hbm.at[part], dst_ref=other_hidden.at[part],
             send_sem=hid_send.at[i], recv_sem=hid_recv.at[i],
             device_id=peer, device_id_type=MESH,
         )
 
-    hidden_copies = [send_hidden(i) for i in range(HIDDEN_PIECES)]
+    hidden_copies = [send_hidden(0, 0, FIRST), send_hidden(1, FIRST, rows - FIRST)]
     hidden_copies[0].start()
 
-    centered_x = center_rows(acts_ref[...])
-    centered_y = center_rows(partner_ref[...])
+    loads[0].wait()
+    loads[1].wait()
+    centered_x = center_rows(acts[...])
+    centered_y = center_rows(partner[...])
     grams[0, 0] = token_gram(centered_x)
     grams[0, 1] = token_gram(centered_y)
     gram_copy = pltpu.make_async_remote_copy(
@@ -84,8 +96,7 @@
         device_id=peer, device_id_type=MESH,
     )
     gram_copy.start()
-    for copy in hidden_copies[1:]:
-        copy.start()
+    hidden_copies[1].start()
     gram_copy.wait()
     gram_x = grams[0, 0] + grams[1, 0]
     gram_y = grams[0, 1] + grams[1, 1]
@@ -110,17 +121,14 @@
     ratio = sxy / sxx
     coef = -2.0 * scale / root
     mixed = gram_y - ratio * gram_x
-    grad = jnp.zeros(mine.shape, jnp.float32)
+    grad = jnp.zeros(centered_x.shape, jnp.float32)
     rest = mixed
     for _ in range(3):
         top = rest.astype(jnp.bfloat16)
         rest = rest - top.astype(jnp.float32)
         grad += jnp.dot(top, centered_x, preferred_element_type=jnp.float32)
-    mine[...] = (coef * grad).astype(jnp.bfloat16)
-
     own_rows = pl.ds(pl.multiple_of(rows_of(dp), tokens), tokens)
-    own_copy = pltpu.make_async_copy(mine, cols_ref.at[own_rows], own_sem)
-    own_copy.start()
+    cols[own_rows] = (coef * grad).astype(jnp.bfloat16)
 
     last = chips // 2
 
@@ -130,18 +138,18 @@
         if step == last:
             size = tokens // 2
             start = start + (0 if way > 0 else size)
-        rows = pl.ds(pl.multiple_of(start, size), size)
+        span = pl.ds(pl.multiple_of(start, size), size)
         sends, recvs = (up_send, up_recv) if way > 0 else (down_send, down_recv)
         return pltpu.make_async_remote_copy(
-            src_ref=mine if step == 1 else cols_ref.at[rows], dst_ref=cols_ref.at[rows],
+            src_ref=cols.at[span], dst_ref=cols.at[span],
             send_sem=sends.at[step - 1], recv_sem=recvs.at[step - 1],
             device_id=above if way > 0 else below, device_id_type=MESH,
         )
 
     def share(i, block):
-        rows = pl.ds(pl.multiple_of(rows_of(block), tokens), tokens)
+        span = pl.ds(pl.multiple_of(rows_of(block), tokens), tokens)
         return pltpu.make_async_remote_copy(
-            src_ref=mine if i == 0 else cols_ref.at[rows], dst_ref=cols_ref.at[rows],
+            src_ref=cols.at[span], dst_ref=cols.at[span],
             send_sem=sib_send.at[i], recv_sem=sib_recv.at[i],
             device_id=sibling, device_id_type=MESH,
         )
@@ -163,64 +171,114 @@
     shares.append(share(len(shares), device_at(last)))
     shares[-1].start()
 
-    own_copy.wait()
     for copy in ups + downs:
         copy.wait_send()
     for copy in shares:
         copy.wait()
+    loads[2].wait()
+    loads[3].wait()
+
+    half = n_dp * tokens // 2
+    size = rows // PARTS
+    own, other = pl.ds(0, half), pl.ds(half, half)
+
+    def span_of(i):
+        return pl.ds(pl.multiple_of(i * size, 16), size)
+
+    def send_part(i):
+        span = span_of(i)
+        return pltpu.make_async_remote_copy(
+            src_ref=theirs.at[span], dst_ref=arrived.at[span],
+            send_sem=part_send.at[i], recv_sem=part_recv.at[i],
+            device_id=peer, device_id_type=MESH,
+        )
+
+    contract = (((1,), (1,)), ((), ()))
+
+    def half_sum(i, chosen):
+        return lax.dot_general(
+            weight[span_of(i)], cols[chosen], contract, preferred_element_type=jnp.float32
+        )
+
+    @pl.loop(0, PARTS)
+    def _(i):
+        theirs[span_of(i)] = half_sum(i, other).astype(jnp.bfloat16)
+        send_part(i).start()
+
+    @pl.loop(0, PARTS)
+    def _(i):
+        ours[span_of(i)] = half_sum(i, own)
+
     for copy in hidden_copies:
         copy.wait()
 
-
-def gather(acts, partner, hidden, scale):
+    @pl.loop(0, cols.shape[1] // TILE)
+    def _(i):
+        span = pl.ds(pl.multiple_of(i * TILE, TILE), TILE)
+        grad_weight[:, span] = jnp.dot(
+            hidden[...], cols[own, span], preferred_element_type=jnp.float32
+        ) + jnp.dot(other_hidden[...], cols[other, span], preferred_element_type=jnp.float32)
+
+    store_weight = pltpu.make_async_copy(grad_weight, grad_weight_hbm, weight_sem)
+    store_weight.start()
+
+    def store(i):
+        return pltpu.make_async_copy(
+            grad_hidden.at[span_of(i)], grad_hidden_hbm.at[span_of(i)], store_sem.at[i]
+        )
+
+    @pl.loop(0, PARTS)
+    def _(i):
+        span = span_of(i)
+        send_part(i).wait_recv()
+        grad_hidden[span] = (ours[span] + arrived[span].astype(jnp.float32)).astype(jnp.bfloat16)
+        store(i).start()
+
+    @pl.loop(0, PARTS)
+    def _(i):
+        send_part(i).wait_send()
+        store(i).wait()
+
+    store_weight.wait()
+
+
+def paired(acts, partner, hidden, down_weight):
     n_dp = lax.axis_size("dp")
     tokens, width = acts.shape
+    rows, half = hidden.shape
+    scale = float(tokens * n_dp * width * lax.axis_size("tensor"))
     rounds = n_dp.bit_length() - 1
     steps = n_dp // 4
-    dma = pltpu.SemaphoreType.DMA
-    vmem, anywhere = pl.BlockSpec(memory_space=pltpu.VMEM), pl.BlockSpec(memory_space=pl.ANY)
-    return pl.pallas_call(
-        functools.partial(gather_kernel, n_dp, scale),
+    dma, bf16, f32 = pltpu.SemaphoreType.DMA, jnp.bfloat16, jnp.float32
+    vmem, hbm = pl.BlockSpec(memory_space=pltpu.VMEM), pl.BlockSpec(memory_space=pltpu.HBM)
+    grad_hidden, grad_weight, cka = pl.pallas_call(
+        functools.partial(fused_kernel, n_dp, scale),
         out_shape=(
-            jax.ShapeDtypeStruct((n_dp * tokens, width), jnp.bfloat16),
-            jax.ShapeDtypeStruct(hidden.shape, jnp.bfloat16),
-            jax.ShapeDtypeStruct((8, 128), jnp.float32),
+            jax.ShapeDtypeStruct((rows, half), bf16),
+            jax.ShapeDtypeStruct((rows, width), f32),
+            jax.ShapeDtypeStruct((8, 128), f32),
         ),
-        in_specs=[vmem, vmem, anywhere],
-        out_specs=(anywhere, anywhere, vmem),
+        in_specs=[hbm] * 4,
+        out_specs=(hbm, hbm, vmem),
         scratch_shapes=[
-            pltpu.VMEM((2, 2, tokens, tokens), jnp.float32),
-            pltpu.VMEM((2 * rounds + 1, 8, tokens), jnp.float32),
-            pltpu.VMEM((tokens, width), jnp.bfloat16),
-            dma((HIDDEN_PIECES,)), dma((HIDDEN_PIECES,)), dma, dma,
-            dma((rounds,)), dma((rounds,)),
+            pltpu.VMEM((tokens, width), bf16), pltpu.VMEM((tokens, width), bf16),
+            pltpu.VMEM((rows, half), bf16), pltpu.VMEM((rows, width), bf16),
+            pltpu.VMEM((rows, half), bf16), pltpu.VMEM((n_dp * tokens, width), bf16),
+            pltpu.VMEM((rows, half), bf16), pltpu.VMEM((rows, half), bf16),
+            pltpu.VMEM((rows, half), f32), pltpu.VMEM((rows, half), bf16), pltpu.VMEM((rows, width), f32),
+            pltpu.VMEM((2, 2, tokens, tokens), f32),
+            pltpu.VMEM((2 * rounds + 1, 8, tokens), f32),
+            dma((4,)), dma, dma((PARTS,)), dma((2,)), dma((2,)), dma, dma, dma((rounds,)), dma((rounds,)),
             dma((steps,)), dma((steps,)), dma((steps,)), dma((steps,)),
-            dma((2 * steps,)), dma((2 * steps,)), dma,
+            dma((2 * steps,)), dma((2 * steps,)), dma((PARTS,)), dma((PARTS,)),
         ],
         compiler_params=pltpu.CompilerParams(
-            collective_id=0, has_side_effects=True, vmem_limit_bytes=32 * 2**20
+            collective_id=0, has_side_effects=True, vmem_limit_bytes=56 * 2**20
         ),
-    )(acts, partner, hidden)
-
-
-def paired(acts, partner, hidden, down_weight):
-    tokens = acts.shape[0]
-    width = acts.shape[1] * lax.axis_size("tensor")
-    scale = float(tokens * lax.axis_size("dp") * width)
-    cols, other_hidden, cka = gather(acts, partner, hidden, scale)
-    half = cols.shape[0] // 2
-    own, other = cols[:half], cols[half:]
-    contract = (((1,), (1,)), ((), ()))
-    theirs = lax.dot_general(
-        down_weight, other, contract, preferred_element_type=jnp.float32
-    ).astype(jnp.bfloat16)
-    arrived = lax.ppermute(theirs, "tensor", [(0, 1), (1, 0)])
-    ours = lax.dot_general(down_weight, own, contract, preferred_element_type=jnp.float32)
-    grad_weight = jnp.dot(hidden, own, preferred_element_type=jnp.float32) + jnp.dot(
-        other_hidden, other, preferred_element_type=jnp.float32
-    )
-    ours, grad_weight, arrived = lax.optimization_barrier((ours, grad_weight, arrived))
-    grad_hidden = (ours + arrived.astype(jnp.float32)).astype(jnp.bfloat16)
+        cost_estimate=pl.CostEstimate(
+            flops=8 * rows * half * width, transcendentals=0, bytes_accessed=16 * rows * width
+        ),
+    )(acts, partner, hidden, down_weight)
     return (grad_hidden, grad_weight, cka[0, 0])
 
 

time: 112 us -> 99.8 us (0.89)
  Pallas kernels: 52 us -> 92.9 us
  waiting for transfers between devices: 32 us -> 0 us
  matrix products: 11.4 us -> 0 us
  local copies, waits for them, and re-layouts: 12.8 us -> 6.05 us
  other arithmetic: 1.57 us -> 0 us
    pallas_call x1, Pallas kernels: 52 us -> 92.9 us  [paired(): pl.pallas_call(functools.partial(fused_kernel, n_dp, scale), out_shape=(j...]
    ppermute x1 -> x0, waiting for transfers between devices: 32 us -> none  [paired(): arrived = lax.ppermute(theirs, 'tensor', [(0, 1), (1, 0)])]
    dot_general x4 -> x0, matrix products: 11.4 us -> none  [the longest x1 4.22 us: paired(): jnp.dot(hidden, own, preferred_element_type=jnp.float32)]
    unnamed x10 -> x4, local copies, waits for them, and re-layouts: 12.3 us -> 4.87 us
    convert_element_type x1 -> x0, other arithmetic: 1.57 us -> none  [paired(): grad_hidden = (ours + arrived.astype(jnp.float32)).astype(jnp.bfloat16)]
  transfers between devices with their start and end apart: 1 -> 0, of which waited for: 1 -> 0; matrix products, arithmetic and copies ran while one was open for 9% -> 0% of each run, Pallas kernels for 0% -> 0%
where the time goes in v3:
time: 99.8 us; the launch traced here: 99.6 us
  Pallas kernels  92.9 us (93%)
  local copies, waits for them, and re-layouts  6.05 us (6%)
    pallas_call x1, Pallas kernels, paired(): pl.pallas_call(functools.partial(fused_kernel, n_dp, scale), out_shape=(j...  92.9 us
    unnamed x4, local copies, waits for them, and re-layouts  4.87 us

profile of v3, /device:TPU:0, one launch (start us, length us, event | category | flops | bytes accessed | tf_op | source)
XLA Modules:
  0.0 99.6 jit_solution(16357214104256207119)
XLA Ops:
  0.6 92.9 %shard_map.67 = (bf16[896,1024]{1,0:T(8,128)(2,1)}, f32[896,1024]{1,0:T(8,128)}, f32[8,128]{1,0:T(8,128)}) custom-call(bf16[128,1024]{1,0:T(8,128)(2,1)} %acts_hbm.1, bf16[128,1024]{1,0:T(8,128)(2,1)} %partner_hbm.1, bf16[896,1024]{1,0:T(8,128)(2,1)} %hidden_hbm.1, bf16[896,1024]{1,0:T(8,128)(2,1)} %weight_hbm.1), custom_call_target="tpu_custom_call" | custom-call | flops 7516192768 | bytes 14680064 | tf_op jit(solution)/shard_map/pallas_call | solution.py:254
  93.5 1.2 %slice.3 = f32[1,1]{1,0:T(1,128)} slice(f32[8,128]{1,0:T(8,128)} %get-tuple-element.8), slice={[0:1], [0:1]} | slice | bytes 8 | tf_op jit(solution)/shard_map/slice | solution.py:282
  94.7 0.0 copy-start
  94.7 3.0 %copy.9 = bf16[896,1024]{1,0:T(8,128)(2,1)} copy(bf16[896,1024]{1,0:T(8,128)(2,1)} %get-tuple-element.12) | data formatting | bytes 3670016
  97.7 0.0 copy-done
  97.7 1.8 %copy.10 = f32[896,1024]{1,0:T(8,128)} copy(f32[896,1024]{1,0:T(8,128)S(1)} %copy-done) | data formatting | bytes 7340032
Async XLA Ops:
  94.7 3.0 %copy-start = (f32[896,1024]{1,0:T(8,128)S(1)}, f32[896,1024]{1,0:T(8,128)}, u32[]{:S(2)}) copy-start(f32[896,1024]{1,0:T(8,128)} %get-tuple-element.13) | copy-start | bytes 11010052

commit v4 on v3

--- a/solution.py
+++ b/solution.py
@@ -9,7 +9,7 @@
 
 MESH = pl.DeviceIdType.MESH
 FIRST = 64
-PARTS = 4
+PARTS = 7
 TILE = 256
 
 
@@ -117,7 +117,7 @@
     sums = jnp.sum(stats[2 * len(rounds)], axis=1, keepdims=True)
     sxx, syy, sxy = sums[0:1], sums[1:2], sums[2:3]
     root = jnp.sqrt(sxx * syy)
-    cka_ref[...] = jnp.broadcast_to(sxy / root, cka_ref.shape)
+    cka_ref[...] = sxy / root
     ratio = sxy / sxx
     coef = -2.0 * scale / root
     mixed = gram_y - ratio * gram_x
@@ -256,7 +256,7 @@
         out_shape=(
             jax.ShapeDtypeStruct((rows, half), bf16),
             jax.ShapeDtypeStruct((rows, width), f32),
-            jax.ShapeDtypeStruct((8, 128), f32),
+            jax.ShapeDtypeStruct((1, 1), f32),
         ),
         in_specs=[hbm] * 4,
         out_specs=(hbm, hbm, vmem),
@@ -279,7 +279,7 @@
             flops=8 * rows * half * width, transcendentals=0, bytes_accessed=16 * rows * width
         ),
     )(acts, partner, hidden, down_weight)
-    return (grad_hidden, grad_weight, cka[0, 0])
+    return (grad_hidden, grad_weight, cka.reshape(()))
 
 
 def gathered(acts, partner, hidden, down_weight):

time: 99.8 us -> 100 us (level)
  between operations: 0.64 us -> 2.4 us
  local copies, waits for them, and re-layouts: 6.05 us -> 4.87 us
    slice x1 -> x0, local copies, waits for them, and re-layouts: 1.19 us -> none  [paired(): return (grad_hidden, grad_weight, cka[0, 0])]
where the time goes in v4:
time: 100 us
  Pallas kernels  92.8 us (93%)
  local copies, waits for them, and re-layouts  4.87 us (5%)
  between operations  2.4 us (2%)
    pallas_call x1, Pallas kernels, paired(): pl.pallas_call(functools.partial(fused_kernel, n_dp, scale), out_shape=(j...  92.8 us
    unnamed x4, local copies, waits for them, and re-layouts  4.87 us

profile of v4, /device:TPU:0, one launch (start us, length us, event | category | flops | bytes accessed | tf_op | source)
XLA Modules:
  0.0 100.1 jit_solution(17769093737691309985)
XLA Ops:
  0.6 92.8 %shard_map.67 = (bf16[896,1024]{1,0:T(8,128)(2,1)}, f32[896,1024]{1,0:T(8,128)}, f32[1,1]{1,0:T(1,128)}) custom-call(bf16[128,1024]{1,0:T(8,128)(2,1)} %acts_hbm.1, bf16[128,1024]{1,0:T(8,128)(2,1)} %partner_hbm.1, bf16[896,1024]{1,0:T(8,128)(2,1)} %hidden_hbm.1, bf16[896,1024]{1,0:T(8,128)(2,1)} %weight_hbm.1), custom_call_target="tpu_custom_call" | custom-call | flops 7516192768 | bytes 14680064 | tf_op jit(solution)/shard_map/pallas_call | solution.py:254
  93.4 0.0 copy-start
  93.4 3.0 %copy.10 = bf16[896,1024]{1,0:T(8,128)(2,1)} copy(bf16[896,1024]{1,0:T(8,128)(2,1)} %get-tuple-element.12) | data formatting | bytes 3670016
  96.5 0.0 copy-done
  96.5 1.8 %copy.11 = f32[896,1024]{1,0:T(8,128)} copy(f32[896,1024]{1,0:T(8,128)S(1)} %copy-done) | data formatting | bytes 7340032
Async XLA Ops:
  93.4 3.0 %copy-start = (f32[896,1024]{1,0:T(8,128)S(1)}, f32[896,1024]{1,0:T(8,128)}, u32[]{:S(2)}) copy-start(f32[896,1024]{1,0:T(8,128)} %get-tuple-element.13) | copy-start | bytes 11010052
